TPU v7x, 512 devices: a whole 4x8x8 slice. The times are simulated.
512 devices in a mesh: blk: 128 (over x, z_lo, y, core), rows: 4 (over z_hi).
Axes of the slice: x: 4, y: 8, z: 8 (z_hi: 4, z_lo: 2; z = z_hi * 2 + z_lo), core: 2. Of those that a mesh axis runs over, the one named last changes fastest.
Arguments:
- weight: bfloat16 [1024, 16384], P('blk', 'rows')
- factor: bfloat16 [16384, 16384], P('rows', 'blk')
- pairing: int32 [4, 64], replicated, may hold values from 0 to 63, each once within a row
Outputs:
- rotated: float32 [1024, 16384], P('rows', 'blk')
- right_factor: float32 [16384, 16384], P('rows', 'blk')
Inputs may be any that keep to these rules, and one draw needn't show every extreme that they name: Each row of pairing lists every column index of a block once.
All inputs are finite; a program needn't handle non-finite values.
Results may differ from a plain program's by a relative error of at most 0.0003.
Values may be sent and summed in bfloat16 or wider, within the bound.
A program may use at most 64 MiB of HBM per device.

v0:
```python
import jax
import jax.numpy as jnp
from jax import lax
from jax.sharding import PartitionSpec as P

BLOCK = 64
STEPS = 4


def shifted(x, axis, by):
    count = lax.axis_size(axis)
    return lax.ppermute(x, axis, [(i, (i + by) % count) for i in range(count)])


def turn_pair(upper_cols, lower_cols, upper_factor, lower_factor, pair_order):
    columns = pair_order.shape[0]
    ladder = lax.broadcasted_iota(jnp.int32, (columns, columns), 0)
    targets = lax.broadcasted_iota(jnp.int32, (columns, columns), 1)
    matches = (pair_order[:, None] == targets).astype(jnp.int32)
    inverse = jnp.sum(matches * ladder, axis=0)
    partner = jnp.take(lower_cols, pair_order, axis=0)
    partner_factor = jnp.take(lower_factor, pair_order, axis=0)
    upper_norm = jnp.sum(upper_cols * upper_cols, axis=1)
    lower_norm = jnp.sum(partner * partner, axis=1)
    cross_term = jnp.sum(upper_cols * partner, axis=1)
    upper_norm, lower_norm, cross_term = lax.psum((upper_norm, lower_norm, cross_term), "rows")
    rotation_angle = 0.5 * jnp.arctan2(2.0 * cross_term, upper_norm - lower_norm)
    cosine = jnp.cos(rotation_angle)[:, None]
    sine_part = jnp.sin(rotation_angle)[:, None]
    new_upper = cosine * upper_cols + sine_part * partner
    new_partner = cosine * partner - sine_part * upper_cols
    new_upper_factor = cosine * upper_factor + sine_part * partner_factor
    new_partner_factor = cosine * partner_factor - sine_part * upper_factor
    return (
        new_upper,
        jnp.take(new_partner, inverse, axis=0),
        new_upper_factor,
        jnp.take(new_partner_factor, inverse, axis=0),
    )


def per_device(weight, factor, pairing):
    partial_cols = lax.dot_general(
        factor,
        lax.all_gather(weight, "blk", axis=0, tiled=True),
        (((0,), (1,)), ((), ())),
        preferred_element_type=jnp.float32,
    )
    whitened = lax.psum_scatter(partial_cols, "rows", scatter_dimension=1, tiled=True)
    upper_cols = whitened[:BLOCK, :]
    lower_cols = whitened[BLOCK:, :]
    right_cols = factor.astype(jnp.float32).T
    upper_factor = right_cols[:BLOCK, :]
    lower_factor = right_cols[BLOCK:, :]
    for step_index in range(STEPS):
        if step_index > 0:
            upper_cols, upper_factor = shifted((upper_cols, upper_factor), "blk", 1)
            lower_cols, lower_factor = shifted((lower_cols, lower_factor), "blk", -1)
        upper_cols, lower_cols, upper_factor, lower_factor = turn_pair(
            upper_cols, lower_cols, upper_factor, lower_factor, pairing[step_index]
        )
    rotated = jnp.concatenate([upper_cols, lower_cols], axis=0)
    right_factor = jnp.concatenate([upper_factor, lower_factor], axis=0)
    return (rotated.T, right_factor.T)


def solution(mesh):
    in_specs = (P("blk", "rows"), P("rows", "blk"), P())
    out_specs = (P("rows", "blk"), P("rows", "blk"))
    return jax.shard_map(
        per_device, mesh=mesh, in_specs=in_specs, out_specs=out_specs, check_vma=False
    )
```

profile of v0, /device:TPU:128, one launch (start us, length us, event | category | flops | bytes accessed | tf_op | source)
XLA Modules:
  0.0 416.7 jit_solution(13958710799210260204)
XLA Ops:
  8.0 2.3 copy.8
  12.0 223.4 %all-gather.2.cloned.1.call-done = bf16[1024,4096]{1,0:T(8,128)(2,1)} async-done(((bf16[8,4096]{1,0:T(8,128)(2,1)}), bf16[1024,4096]{1,0:T(8,128)(2,1)}) %all-gather.2.cloned.1.call-update) | async-done | bytes 8388624 | tf_op jit(solution)/shard_map/all_gather | solution.py:45
  235.5 7.1 %fusion.4 = f32[128,1024]{1,0:T(8,128)} fusion(bf16[4096,128]{1,0:T(8,128)(2,1)S(1)} %copy-done, bf16[1024,4096]{1,0:T(8,128)(2,1)} %all-gather.2.cloned.1.call-done), kind=kOutput, calls=%fused_computation.99 | convolution fusion | flops 1073741824 | bytes 9961472 | tf_op jit(solution)/shard_map/dot_general | solution.py:43
  244.7 28.6 %reduce-scatter.2.cloned.1.call-done = f32[128,256]{1,0:T(8,128)} async-done(((f32[128,1024]{1,0:T(8,128)}), f32[128,256]{1,0:T(8,128)}) %reduce-scatter.2.cloned.1.call-update) | async-done | bytes 131088 | tf_op jit(solution)/shard_map/reduce_scatter | solution.py:49
  275.9 9.7 %all-reduce.3 = (f32[64]{0:T(128)S(1)}, f32[64]{0:T(128)S(1)}, f32[64]{0:T(128)S(1)}) all-reduce(f32[64]{0:T(128)S(1)} %get-tuple-element.9, f32[64]{0:T(128)S(1)} %get-tuple-element.16, f32[64]{0:T(128)S(1)} %get-tuple-element.8), channel_id=1, replica_groups=mesh['blk'=128,'rows'=4] {'rows'}, use_global_device_ids=true, to_apply=%region_4.6 | all-reduce | flops 192 | bytes 1536 | tf_op jit(solution)/shard_map/psum | solution.py:26
  285.7 2.5 multiply_subtract_fusion.3
  290.4 2.8 collective-permute-start.7
  293.2 1.9 collective-permute-start.6
  296.0 7.9 %collective-permute-start.1 = (f32[64,256]{1,0:T(8,128)S(1)}, f32[64,256]{1,0:T(8,128)S(1)}, u32[]{:S(2)}, u32[]{:S(2)}) collective-permute-start(f32[64,256]{1,0:T(8,128)S(1)} %broadcast_select_fusion.7), channel_id=1, source_target_pairs={{0,508},{4,0},{8,4},{12,8},{16,12},{20,16},{24,20},{28,24},{32,28}... | collective-permute-start | bytes 196616 | tf_op jit(solution)/shard_map/ppermute | solution.py:12
  303.9 1.9 collective-permute-start
  307.1 7.2 %collective-permute-done = f32[64,256]{1,0:T(8,128)S(1)} collective-permute-done((f32[64,256]{1,0:T(8,128)S(1)}, f32[64,256]{1,0:T(8,128)S(1)}, u32[]{:S(2)}, u32[]{:S(2)}) %collective-permute-start) | collective-permute-done | bytes 65568 | tf_op jit(solution)/shard_map/ppermute | solution.py:12
  314.5 11.2 %all-reduce.2 = (f32[64]{0:T(128)S(1)}, f32[64]{0:T(128)S(1)}, f32[64]{0:T(128)S(1)}) all-reduce(f32[64]{0:T(128)S(1)} %get-tuple-element.19, f32[64]{0:T(128)S(1)} %get-tuple-element.15, f32[64]{0:T(128)S(1)} %get-tuple-element.14), channel_id=1, replica_groups=mesh['blk'=128,'rows'=4] {'rows'}, use_global_device_ids=true, to_apply=%region_11.13 | all-reduce | flops 192 | bytes 1536 | tf_op jit(solution)/shard_map/psum | solution.py:26
  330.3 1.9 collective-permute-start.9
  332.3 2.4 collective-permute-start.8
  335.5 7.4 %collective-permute-start.3 = (f32[64,256]{1,0:T(8,128)S(1)}, f32[64,256]{1,0:T(8,128)S(1)}, u32[]{:S(2)}, u32[]{:S(2)}) collective-permute-start(f32[64,256]{1,0:T(8,128)S(1)} %broadcast_select_fusion.6), channel_id=1, source_target_pairs={{0,508},{4,0},{8,4},{12,8},{16,12},{20,16},{24,20},{28,24},{32,28}... | collective-permute-start | bytes 196616 | tf_op jit(solution)/shard_map/ppermute | solution.py:12
  342.9 1.9 collective-permute-start.2
  346.1 7.2 %collective-permute-done.2 = f32[64,256]{1,0:T(8,128)S(1)} collective-permute-done((f32[64,256]{1,0:T(8,128)S(1)}, f32[64,256]{1,0:T(8,128)S(1)}, u32[]{:S(2)}, u32[]{:S(2)}) %collective-permute-start.2) | collective-permute-done | bytes 65568 | tf_op jit(solution)/shard_map/ppermute | solution.py:12
  353.6 9.9 %all-reduce.1 = (f32[64]{0:T(128)S(1)}, f32[64]{0:T(128)S(1)}, f32[64]{0:T(128)S(1)}) all-reduce(f32[64]{0:T(128)S(1)} %get-tuple-element.18, f32[64]{0:T(128)S(1)} %get-tuple-element.13, f32[64]{0:T(128)S(1)} %get-tuple-element.12), channel_id=1, replica_groups=mesh['blk'=128,'rows'=4] {'rows'}, use_global_device_ids=true, to_apply=%region_18.20 | all-reduce | flops 192 | bytes 1536 | tf_op jit(solution)/shard_map/psum | solution.py:26
  369.0 1.9 collective-permute-start.11
  370.9 2.4 collective-permute-start.10
  373.4 7.4 %collective-permute-start.5 = (f32[64,256]{1,0:T(8,128)S(1)}, f32[64,256]{1,0:T(8,128)S(1)}, u32[]{:S(2)}, u32[]{:S(2)}) collective-permute-start(f32[64,256]{1,0:T(8,128)S(1)} %broadcast_select_fusion.5), channel_id=1, source_target_pairs={{0,508},{4,0},{8,4},{12,8},{16,12},{20,16},{24,20},{28,24},{32,28}... | collective-permute-start | bytes 196616 | tf_op jit(solution)/shard_map/ppermute | solution.py:12
  380.8 1.9 collective-permute-start.4
  384.8 7.3 %collective-permute-done.4 = f32[64,256]{1,0:T(8,128)S(1)} collective-permute-done((f32[64,256]{1,0:T(8,128)S(1)}, f32[64,256]{1,0:T(8,128)S(1)}, u32[]{:S(2)}, u32[]{:S(2)}) %collective-permute-start.4) | collective-permute-done | bytes 65568 | tf_op jit(solution)/shard_map/ppermute | solution.py:12
  392.2 10.3 %all-reduce = (f32[64]{0:T(128)S(1)}, f32[64]{0:T(128)S(1)}, f32[64]{0:T(128)S(1)}) all-reduce(f32[64]{0:T(128)S(1)} %get-tuple-element.17, f32[64]{0:T(128)S(1)} %get-tuple-element.11, f32[64]{0:T(128)S(1)} %get-tuple-element.10), channel_id=1, replica_groups=mesh['blk'=128,'rows'=4] {'rows'}, use_global_device_ids=true, to_apply=%region_25.27 | all-reduce | flops 192 | bytes 1536 | tf_op jit(solution)/shard_map/psum | solution.py:26
  (93 shorter events, 33.7 us)
Async XLA Ops:
  7.2 3.1 copy-start.3
  7.2 228.3 %all-gather.2.cloned.1.call-start = ((), (), s32[]{:S(2)}) async-start(), calls=%async_computation.1 | async-start | bytes 8454144 | tf_op jit(solution)/shard_map/all_gather | solution.py:45
  7.9 265.4 %reduce-scatter.2.cloned.1.call-start = ((), (), s32[]{:S(2)}) async-start(), calls=%async_computation.2 | async-start | bytes 655360 | tf_op jit(solution)/shard_map/reduce_scatter | solution.py:49
  10.2 225.2 %copy-start = (bf16[4096,128]{1,0:T(8,128)(2,1)S(1)}, bf16[4096,128]{1,0:T(8,128)(2,1)}, u32[]{:S(2)}) copy-start(bf16[4096,128]{1,0:T(8,128)(2,1)} %param.8) | copy-start | bytes 3145732
  289.2 4.0 copy-start.1
  289.2 6.0 %copy-start.2 = (f32[128,256]{1,0:T(8,128)S(1)}, f32[128,256]{1,0:T(8,128)}, u32[]{:S(2)}) copy-start(f32[128,256]{1,0:T(8,128)} %reduce-scatter.2.cloned.1.call-done) | copy-start | bytes 393220
  290.4 35.4 %collective-permute-start.7 = (f32[64,4096]{1,0:T(8,128)}, f32[64,4096]{1,0:T(8,128)S(1)}, u32[]{:S(2)}, u32[]{:S(2)}) collective-permute-start(f32[64,4096]{1,0:T(8,128)} %broadcast_select_fusion.3), channel_id=1, source_target_pairs={{0,508},{4,0},{8,4},{12,8},{16,12},{20,16},{24,20},{28,24},{32,28}... | collective-permute-start | bytes 3145736 | tf_op jit(solution)/shard_map/ppermute | solution.py:12
  293.2 33.5 %collective-permute-start.6 = (f32[64,4096]{1,0:T(8,128)S(1)}, f32[64,4096]{1,0:T(8,128)}, u32[]{:S(2)}, u32[]{:S(2)}) collective-permute-start(f32[64,4096]{1,0:T(8,128)S(1)} %copy-done.1), channel_id=1, source_target_pairs={{0,4},{4,8},{8,12},{12,16},{16,20},{20,24},{24,28},{28,32},{32,36}... | collective-permute-start | bytes 3145736 | tf_op jit(solution)/shard_map/ppermute | solution.py:12
  296.0 10.4 %collective-permute-start.1 = (f32[64,256]{1,0:T(8,128)S(1)}, f32[64,256]{1,0:T(8,128)S(1)}, u32[]{:S(2)}, u32[]{:S(2)}) collective-permute-start(f32[64,256]{1,0:T(8,128)S(1)} %broadcast_select_fusion.7), channel_id=1, source_target_pairs={{0,508},{4,0},{8,4},{12,8},{16,12},{20,16},{24,20},{28,24},{32,28}... | collective-permute-start | bytes 196616 | tf_op jit(solution)/shard_map/ppermute | solution.py:12
  303.9 10.4 %collective-permute-start = (f32[64,256]{1,0:T(8,128)S(1)}, f32[64,256]{1,0:T(8,128)S(1)}, u32[]{:S(2)}, u32[]{:S(2)}) collective-permute-start(f32[64,256]{1,0:T(8,128)S(1)} %get-tuple-element.57), channel_id=1, source_target_pairs={{0,4},{4,8},{8,12},{12,16},{16,20},{20,24},{24,28},{28,32},{32,36}... | collective-permute-start | bytes 196616 | tf_op jit(solution)/shard_map/ppermute | solution.py:12
  330.3 34.1 %collective-permute-start.9 = (f32[64,4096]{1,0:T(8,128)}, f32[64,4096]{1,0:T(8,128)S(1)}, u32[]{:S(2)}, u32[]{:S(2)}) collective-permute-start(f32[64,4096]{1,0:T(8,128)} %broadcast_select_fusion.2), channel_id=1, source_target_pairs={{0,508},{4,0},{8,4},{12,8},{16,12},{20,16},{24,20},{28,24},{32,28}... | collective-permute-start | bytes 3145736 | tf_op jit(solution)/shard_map/ppermute | solution.py:12
  332.3 33.1 %collective-permute-start.8 = (f32[64,4096]{1,0:T(8,128)S(1)}, f32[64,4096]{1,0:T(8,128)}, u32[]{:S(2)}, u32[]{:S(2)}) collective-permute-start(f32[64,4096]{1,0:T(8,128)S(1)} %get-tuple-element.55), channel_id=1, source_target_pairs={{0,4},{4,8},{8,12},{12,16},{16,20},{20,24},{24,28},{28,32},{32,36}... | collective-permute-start | bytes 3145736 | tf_op jit(solution)/shard_map/ppermute | solution.py:12
  335.5 10.0 %collective-permute-start.3 = (f32[64,256]{1,0:T(8,128)S(1)}, f32[64,256]{1,0:T(8,128)S(1)}, u32[]{:S(2)}, u32[]{:S(2)}) collective-permute-start(f32[64,256]{1,0:T(8,128)S(1)} %broadcast_select_fusion.6), channel_id=1, source_target_pairs={{0,508},{4,0},{8,4},{12,8},{16,12},{20,16},{24,20},{28,24},{32,28}... | collective-permute-start | bytes 196616 | tf_op jit(solution)/shard_map/ppermute | solution.py:12
  342.9 10.5 %collective-permute-start.2 = (f32[64,256]{1,0:T(8,128)S(1)}, f32[64,256]{1,0:T(8,128)S(1)}, u32[]{:S(2)}, u32[]{:S(2)}) collective-permute-start(f32[64,256]{1,0:T(8,128)S(1)} %get-tuple-element.63), channel_id=1, source_target_pairs={{0,4},{4,8},{8,12},{12,16},{16,20},{20,24},{24,28},{28,32},{32,36}... | collective-permute-start | bytes 196616 | tf_op jit(solution)/shard_map/ppermute | solution.py:12
  369.0 35.3 %collective-permute-start.11 = (f32[64,4096]{1,0:T(8,128)}, f32[64,4096]{1,0:T(8,128)S(1)}, u32[]{:S(2)}, u32[]{:S(2)}) collective-permute-start(f32[64,4096]{1,0:T(8,128)} %broadcast_select_fusion.1), channel_id=1, source_target_pairs={{0,508},{4,0},{8,4},{12,8},{16,12},{20,16},{24,20},{28,24},{32,28}... | collective-permute-start | bytes 3145736 | tf_op jit(solution)/shard_map/ppermute | solution.py:12
  370.9 34.3 %collective-permute-start.10 = (f32[64,4096]{1,0:T(8,128)S(1)}, f32[64,4096]{1,0:T(8,128)}, u32[]{:S(2)}, u32[]{:S(2)}) collective-permute-start(f32[64,4096]{1,0:T(8,128)S(1)} %get-tuple-element.53), channel_id=1, source_target_pairs={{0,4},{4,8},{8,12},{12,16},{16,20},{20,24},{24,28},{28,32},{32,36}... | collective-permute-start | bytes 3145736 | tf_op jit(solution)/shard_map/ppermute | solution.py:12
  373.4 10.7 %collective-permute-start.5 = (f32[64,256]{1,0:T(8,128)S(1)}, f32[64,256]{1,0:T(8,128)S(1)}, u32[]{:S(2)}, u32[]{:S(2)}) collective-permute-start(f32[64,256]{1,0:T(8,128)S(1)} %broadcast_select_fusion.5), channel_id=1, source_target_pairs={{0,508},{4,0},{8,4},{12,8},{16,12},{20,16},{24,20},{28,24},{32,28}... | collective-permute-start | bytes 196616 | tf_op jit(solution)/shard_map/ppermute | solution.py:12
  380.8 11.3 %collective-permute-start.4 = (f32[64,256]{1,0:T(8,128)S(1)}, f32[64,256]{1,0:T(8,128)S(1)}, u32[]{:S(2)}, u32[]{:S(2)}) collective-permute-start(f32[64,256]{1,0:T(8,128)S(1)} %get-tuple-element.61), channel_id=1, source_target_pairs={{0,4},{4,8},{8,12},{12,16},{16,20},{20,24},{24,28},{28,32},{32,36}... | collective-permute-start | bytes 196616 | tf_op jit(solution)/shard_map/ppermute | solution.py:12
Sparse Core Ops, SparseCore 0:
  10.2 225.2 all-gather.1
  242.8 30.5 reduce-scatter.1
where the time goes:
time: 417 us
  waiting for transfers between devices  277 us (66%)
  starting transfers between devices  41.8 us (10%)
  blocking collectives  41.1 us (10%)
  local copies, waits for them, and re-layouts  19.5 us (5%)
  other arithmetic  15.6 us (4%)
  between operations  14.5 us (3%)
  matrix products  7.14 us (2%)
    all_gather x1, waiting for transfers between devices, per_device(): lax.all_gather(weight, 'blk', axis=0, tiled=True)  223 us
    ppermute x12, starting transfers between devices, shifted(): return lax.ppermute(x, axis, [(i, (i + by) % count) for i in range(count)])  41.7 us
    psum x4, blocking collectives, turn_pair(): lax.psum((upper_norm, lower_norm, cross_term), 'rows')  41.1 us
    reduce_scatter x1, waiting for transfers between devices, per_device(): lax.psum_scatter(partial_cols, 'rows', scatter_dimension=1, tiled=True)  28.6 us
    ppermute x12, waiting for transfers between devices, shifted(): return lax.ppermute(x, axis, [(i, (i + by) % count) for i in range(count)])  24.3 us
  transfers between devices with their start and end apart: 14, of which 8 were waited for; matrix products, arithmetic and copies ran while one was open for 4% of the time, Pallas kernels for 0%

commit v1 on v0

v1 whole, which is shorter than its diff:
```python
import functools
import jax
import jax.numpy as jnp
from jax import lax
from jax.experimental import pallas as pl
from jax.experimental.pallas import tpu as pltpu
from jax.sharding import PartitionSpec as P

MESH = pl.DeviceIdType.MESH
BLOCK = 64
STEPS = 4
NX, NZ, NY, NR = 4, 2, 8, 4
NB = 2 * NX * NZ * NY
HOPS = ((1, 0, 0), (3, 0, 0), (0, 1, 0), (0, 0, 1), (0, 0, 7))
TREE = (
    (0, 1, 0, 2), (3, 0, 0, 1), (0, 0, 1, 3), (0, 0, 7, 4), (1, 0, 0, 0), (2, 0, 0, 1), (1, 1, 0, 0), (0, 0, 6, 4),
    (0, 0, 2, 3), (0, 1, 7, 2), (1, 0, 7, 0), (3, 0, 7, 1), (0, 1, 1, 3), (3, 1, 0, 2), (3, 0, 1, 1), (1, 0, 1, 0),
    (1, 1, 7, 4), (0, 1, 6, 2), (0, 0, 3, 3), (2, 1, 0, 0), (3, 1, 7, 1), (1, 0, 6, 4), (0, 1, 2, 3), (2, 0, 7, 0),
    (3, 1, 1, 1), (1, 1, 1, 2), (1, 0, 2, 3), (3, 0, 6, 4), (3, 0, 2, 1), (2, 0, 1, 0), (0, 0, 4, 3), (0, 1, 5, 4),
    (0, 1, 3, 2), (2, 1, 7, 1), (1, 0, 3, 0), (1, 1, 6, 2), (2, 0, 6, 4), (3, 1, 2, 3), (3, 1, 6, 1), (1, 1, 2, 0),
    (2, 0, 2, 3), (3, 0, 5, 4), (2, 1, 1, 2), (3, 0, 3, 1), (1, 1, 5, 0), (0, 1, 4, 2), (2, 1, 6, 4), (3, 0, 4, 1),
    (1, 1, 3, 0), (0, 0, 5, 2), (3, 1, 3, 1), (2, 1, 2, 0), (3, 1, 5, 2), (2, 0, 3, 1), (2, 1, 5, 0), (3, 1, 4, 1),
    (1, 0, 5, 0), (2, 1, 3, 1), (1, 0, 4, 0), (2, 0, 4, 1), (1, 1, 4, 0), (2, 1, 4, 1), (2, 0, 5, 0),
)
PLANES = (0, 3, 1, 2)
LEAVES = tuple((b3, b2, b1) for b3 in (0, 1) for b2 in (0, 1) for b1 in (0, 1))


def plus(offset, hop):
    return tuple((a + b) % n for a, b, n in zip(offset, hop, (NX, NZ, NY)))


def turn(p_minus_r, q):
    y = 2.0 * q
    x = p_minus_r
    top = jnp.maximum(jnp.abs(x), jnp.abs(y))
    safe = jnp.where(top > 0.0, top, 1.0)
    xs = jnp.where(top > 0.0, x / safe, 1.0)
    ys = jnp.where(top > 0.0, y / safe, 0.0)
    h = jnp.sqrt(xs * xs + ys * ys)
    big = jnp.sqrt(0.5 * (1.0 + jnp.abs(xs) / h))
    small = jnp.abs(ys) / (2.0 * h * big)
    cosine = jnp.where(x >= 0.0, big, small)
    size = jnp.where(x >= 0.0, small, big)
    return cosine, jnp.where(y < 0.0, -size, size)


def split3(x):
    hi = x.astype(jnp.bfloat16)
    rest = x - hi.astype(jnp.float32)
    mid = rest.astype(jnp.bfloat16)
    low = (rest - mid.astype(jnp.float32)).astype(jnp.bfloat16)
    return hi, mid, low


def dot(a, b, dims=(((1,), (0,)), ((), ()))):
    return lax.dot_general(a, b, dims, preferred_element_type=jnp.float32)


def gram_plan():
    rows = {}
    for n in range(8):
        rows["pr", n] = len(rows)
        rows["q", n] = len(rows)
    for level in (1, 2, 3):
        for n in range(8):
            for m in range(8):
                if n >> level == m >> level and (n >> (level - 1)) & 1 == 0 and (m >> (level - 1)) & 1 == 1:
                    rows["same", n, m] = len(rows)
                    rows["cross", n, m] = len(rows)
    return rows


GRAM = gram_plan()


def kernel(
    w_ref, f_ref, pair_ref, rot_ref, right_ref,
    wbuf, fbuf, part, rsbuf, wsum, xbuf, ybuf, gram, gbuf, ebuf, mbuf, coef,
    wsend, wrecv, own_sem, fsend, frecv, rssend, rsrecv, xsend, xrecv, gsend, grecv,
):
    b = lax.axis_index("blk")
    r = lax.axis_index("rows")
    core = lax.rem(b, 2)
    y = lax.rem(b // 2, NY)
    z = lax.rem(b // (2 * NY), NZ)
    x = b // (2 * NY * NZ)
    sigma = 1 - 2 * core

    def blk(shift):
        return (lax.rem(b + shift + NB, NB), r)

    def hop(h):
        dx, dz, dy = HOPS[h]
        index = lax.rem(x + dx, NX) * (2 * NY * NZ) + lax.rem(z + dz, NZ) * (2 * NY) + lax.rem(y + dy, NY) * 2 + core
        return (index, r)

    def peer(shift):
        return (b, lax.rem(r + shift, NR))

    own_factor = pltpu.make_async_copy(f_ref, fbuf.at[0], own_sem)
    own_factor.start()

    barrier = pltpu.get_barrier_semaphore()
    greet = [hop(h) for h in range(5)] + [peer(s) for s in (1, 2, 3)]
    greet += [blk(sigma * s) for s in (1, -1, 3, -3, 2, -2, -4)]
    for target in greet:
        pl.semaphore_signal(barrier, inc=1, device_id=target, device_id_type=MESH)

    def remote(src, dst, send, recv, target):
        return pltpu.make_async_remote_copy(
            src_ref=src, dst_ref=dst, send_sem=send, recv_sem=recv, device_id=target, device_id_type=MESH
        )

    def slot(offset):
        return (offset[0] * NZ + offset[1]) * NY + lax.rem(y - offset[2] + NY, NY)

    index_of = {entry[:3]: k for k, entry in enumerate(TREE)}
    children = {}
    for k, entry in enumerate(TREE):
        back = tuple(-v for v in HOPS[entry[3]])
        children.setdefault(plus(entry[:3], back), []).append(k)
    pending = []

    def weight_copy(k):
        offset, h = TREE[k][:3], TREE[k][3]
        source = plus(offset, tuple(-v for v in HOPS[h]))
        line = offset[0] * NZ + offset[1]
        return remote(
            wbuf.at[slot(source)],
            wbuf.at[line * NY + lax.rem(y - source[2] + NY, NY)],
            wsend.at[k],
            wrecv.at[k],
            hop(h),
        )

    def forward(offset):
        for k in children.get(offset, ()):
            copy = weight_copy(k)
            copy.start()
            pending.append(copy)

    def arrived(k):
        weight_copy(k).wait_recv()

    wide = w_ref[...].astype(jnp.float32)
    half = wide.shape[1] // 2
    wbuf[y] = jnp.concatenate([wide[:, :half], wide[:, half:]], axis=0).astype(jnp.bfloat16)

    own_factor.wait()
    pl.semaphore_wait(barrier, len(greet))
    forward((0, 0, 0))
    swap = remote(fbuf.at[0], fbuf.at[1], fsend.at[0], frecv.at[0], blk(sigma))
    swap.start()
    pending.append(swap)

    depth = fbuf.shape[1]
    halves = [pl.ds(0, depth // 2), pl.ds(depth // 2, depth // 2)]

    def factor_out():
        for k, rows in enumerate(halves):
            for base, shift, place in ((1, -1, 2), (3, 3, 4)):
                copy = remote(
                    fbuf.at[0, rows], fbuf.at[place, rows], fsend.at[base + k], frecv.at[base + k], blk(sigma * shift)
                )
                copy.start()
                pending.append(copy)

    waited = set()
    last_parent = max(k for k, entry in enumerate(TREE) if entry[:3] in children)
    for k in range(last_parent + 1):
        if TREE[k][:3] in children:
            arrived(k)
            waited.add(k)
            forward(TREE[k][:3])
        if k == 30:
            factor_out()

    swap.wait_recv()
    kdim = half
    lines = []

    def whiten(line):
        dx, dz = line // NZ, line % NZ
        for dy in range(NY):
            if (dx, dz, dy) != (0, 0, 0) and index_of[dx, dz, dy] not in waited:
                arrived(index_of[dx, dz, dy])
                waited.add(index_of[dx, dz, dy])
        left = wbuf[pl.ds(line * NY, NY)].reshape(NY * 16, kdim)
        total = None
        for side in (0, 1):
            rows = pl.ds(side * kdim, kdim)
            right = jnp.concatenate([fbuf[0, rows, :], fbuf[1, rows, :]], axis=1)
            d = dot(left, right).reshape(NY, 2, 8, 256)[:, side]
            total = d if total is None else total + d
        part[line] = total.reshape(NY * 8, 256)
        ahead = lax.rem(x - dx - r + 2 * NX, NR)
        place = lax.rem(z + dz, NZ)
        index = jnp.maximum(ahead - 1, 0)

        @pl.when(ahead != 0)
        def _():
            remote(
                part.at[line], rsbuf.at[index, place], rssend.at[line], rsrecv.at[index, place], peer(ahead)
            ).start()

        lines.append((line, ahead, index, place))

    for dx in PLANES:
        for dz in range(NZ):
            whiten(dx * NZ + dz)

    for k, rows in enumerate(halves):
        remote(fbuf.at[0, rows], fbuf.at[2, rows], fsend.at[1 + k], frecv.at[1 + k], blk(-sigma)).wait_recv()
        copy = remote(fbuf.at[2, rows], fbuf.at[3, rows], fsend.at[5 + k], frecv.at[5 + k], blk(2 * sigma))
        copy.start()
        pending.append(copy)

    row_id = lax.broadcasted_iota(jnp.int32, (128, 128), 0)
    lane_id = lax.broadcasted_iota(jnp.int32, (128, 128), 1)

    def exact(mask):
        return jnp.where(mask, 1.0, 0.0).astype(jnp.bfloat16)

    turns = [exact(row_id == pair_ref[s : s + 1, :]) for s in range(STEPS)]
    eye = exact(row_id == lane_id)
    swap_halves = exact(lax.rem(row_id + BLOCK, 2 * BLOCK) == lane_id)
    low_lane = lane_id < BLOCK
    first = jnp.where(low_lane, eye.astype(jnp.float32), turns[0].astype(jnp.float32)).astype(jnp.bfloat16)
    last = jnp.where(low_lane, eye.astype(jnp.float32), turns[3].astype(jnp.float32)).astype(jnp.bfloat16)
    across = (((1,), (1,)), ((), ()))
    down = (((0,), (0,)), ((), ()))
    q1, q2, q3 = (dot(turns[s - 1], turns[s], down).astype(jnp.bfloat16) for s in (1, 2, 3))
    for n, (b3, b2, b1) in enumerate(LEAVES):
        m = eye
        for bit, q in ((b3, q3), (b2, q2), (b1, q1)):
            if bit:
                m = dot(q, m).astype(jnp.bfloat16)
        e = dot(first, m)
        es = dot(e.astype(jnp.bfloat16), swap_halves)
        ebuf[n, :, 0:128] = e.astype(jnp.bfloat16)
        ebuf[n, :, 128:256] = es.astype(jnp.bfloat16)
        mbuf[n] = dot((e + es).astype(jnp.bfloat16), last, across)

    for k in range(3):
        for place in range(NZ):
            remote(part.at[0], rsbuf.at[k, place], rssend.at[0], rsrecv.at[k, place], peer(1)).wait_recv()
    for place in range(NZ):
        mine = lax.rem(x - r + NX, NX) * NZ + lax.rem(z + place, NZ)
        total = (part[mine] + rsbuf[0, place]) + (rsbuf[1, place] + rsbuf[2, place])
        wsum[0, place * 64 : place * 64 + 64, :] = total[:, 0:128]
        wsum[1, place * 64 : place * 64 + 64, :] = total[:, 128:256]

    for k, shift in enumerate((1, -1, 3, -3)):
        index = (3 - sigma * shift) // 2
        copy = remote(wsum.at[0], xbuf.at[index, core], xsend.at[k], xrecv.at[index, core], blk(sigma * shift))
        copy.start()
        pending.append(copy)
    for k, shift in enumerate((1, 3, -3)):
        index = (3 - sigma * shift) // 2
        copy = remote(
            wsum.at[1], xbuf.at[index, core], xsend.at[4 + k], xrecv.at[index, core], blk(sigma * (shift + 1))
        )
        copy.start()
        pending.append(copy)
    xbuf[(3 + sigma) // 2, core] = wsum[1]
    for shift in (1, -1, 3, -3):
        index = (3 + sigma * shift) // 2
        remote(wsum.at[0], xbuf.at[index, 1 - core], xsend.at[0], xrecv.at[index, 1 - core], blk(sigma)).wait_recv()
        if shift != 1:
            remote(wsum.at[0], xbuf.at[index, core], xsend.at[0], xrecv.at[index, core], blk(sigma)).wait_recv()

    for i in range(4):
        pieces = split3(xbuf[i].reshape(256, 128))
        for n in range(8):
            if sum(LEAVES[n]) == i:
                e = ebuf[n]
                ybuf[n] = dot(pieces[0], e) + dot(pieces[1], e) + dot(pieces[2], e)

    def put(name, a, c):
        k = GRAM[name]
        gram[k : k + 1, :] = jnp.sum(a * c, axis=0, keepdims=True)

    for n in range(8):
        a = ybuf[n, :, 0:128]
        put(("pr", n), a, a)
        put(("q", n), a, ybuf[n, :, 128:256])
        for m in range(8):
            if ("same", n, m) in GRAM:
                put(("same", n, m), a, ybuf[m, :, 0:128])
                put(("cross", n, m), a, ybuf[m, :, 128:256])
    gbuf[r] = gram[...]
    for shift in (1, 2, 3):
        copy = remote(gram, gbuf.at[r], gsend.at[shift - 1], grecv.at[r], peer(shift))
        copy.start()
        pending.append(copy)
    for shift in (1, 2, 3):
        other = lax.rem(r + shift, NR)
        remote(gram, gbuf.at[other], gsend.at[0], grecv.at[other], peer(shift)).wait_recv()
    gram_sum = (gbuf[0] + gbuf[1]) + (gbuf[2] + gbuf[3])
    gram_roll = pltpu.roll(gram_sum, BLOCK, 1)

    def row(name, rolled=False):
        k = GRAM[name]
        return (gram_roll if rolled else gram_sum)[k : k + 1, :]

    def rotate(node_u, node_l, p, rr, q):
        c, s = turn(p - rr, q)
        names = sorted(set(node_u) | set(node_l))
        up, low = {}, {}
        for name in names:
            if name in node_u and name in node_l:
                up[name] = c * node_u[name] + s * node_l[name]
                low[name] = c * node_l[name] - s * node_u[name]
            elif name in node_u:
                up[name] = c * node_u[name]
                low[name] = -s * node_u[name]
            else:
                up[name] = s * node_l[name]
                low[name] = c * node_l[name]
        cross = 2.0 * c * s * q
        return up, low, c * c * p + cross + s * s * rr, s * s * p - cross + c * c * rr

    def between(k1, k2):
        n, m = k1 // 2, k2 // 2
        if k1 % 2 == 0:
            return row(("same", n, m)) if k2 % 2 == 0 else row(("cross", n, m))
        return row(("cross", n, m), True) if k2 % 2 == 0 else row(("same", n, m), True)

    one = jnp.ones((1, 128), jnp.float32)
    nodes = [
        rotate({2 * n: one}, {2 * n + 1: one}, row(("pr", n)), row(("pr", n), True), row(("q", n))) for n in range(8)
    ]
    for level in (1, 2, 3):
        grown = []
        for k in range(0, len(nodes), 2):
            up, low = nodes[k][0], nodes[k + 1][1]
            q = None
            for k1, c1 in up.items():
                inner = None
                for k2, c2 in low.items():
                    term = c2 * between(k1, k2)
                    inner = term if inner is None else inner + term
                q = c1 * inner if q is None else q + c1 * inner
            grown.append(rotate(up, low, nodes[k][2], nodes[k + 1][3], q))
        nodes = grown
    up, low = nodes[0][0], nodes[0][1]
    low_row = lax.broadcasted_iota(jnp.int32, (1, 128), 1) < BLOCK
    for k in range(16):
        coef[k : k + 1, :] = jnp.where(low_row, up[k], pltpu.roll(low[k], BLOCK, 1))
    spread = sum(dot(piece, last, across) for piece in split3(coef[...]))
    upper_rows = row_id < BLOCK
    t = [None] * 4
    for n in range(8):
        term = mbuf[n] * jnp.where(upper_rows, spread[2 * n : 2 * n + 1, :], spread[2 * n + 1 : 2 * n + 2, :])
        i = sum(LEAVES[n])
        t[i] = term if t[i] is None else t[i] + term

    rotated = None
    pieces_t = [split3(v) for v in t]
    for i in range(4):
        xs = split3(xbuf[i].reshape(256, 128))
        for a in range(3):
            for c in range(3 - a):
                term = dot(xs[a], pieces_t[i][c])
                rotated = term if rotated is None else rotated + term
    for c in range(2):
        rot_ref[:, c] = rotated[c * 128 : c * 128 + 128].reshape(16, 8, 128)

    pair_t = [jnp.concatenate([v[0], v[1]], axis=1) for v in pieces_t]
    even = core == 0

    def choose(a, c):
        return jnp.where(even, a.astype(jnp.float32), c.astype(jnp.float32)).astype(jnp.bfloat16)

    t_cat = jnp.concatenate(
        [
            choose(pair_t[2], pair_t[1]),
            choose(pair_t[1], pair_t[2]),
            choose(pair_t[0], pair_t[3]),
            choose(pair_t[3], pair_t[0]),
        ],
        axis=0,
    )
    for k in range(2):
        remote(fbuf.at[0, halves[k]], fbuf.at[4, halves[k]], fsend.at[3 + k], frecv.at[3 + k], blk(sigma)).wait_recv()
        remote(fbuf.at[2, halves[k]], fbuf.at[3, halves[k]], fsend.at[5 + k], frecv.at[5 + k], blk(sigma)).wait_recv()

    def turn_rows(k, carry):
        rows = pl.ds(pl.multiple_of(k * 256, 256), 256)
        left = jnp.concatenate([fbuf[s, rows, :] for s in (1, 2, 3, 4)], axis=1)
        d = dot(left, t_cat)
        right_ref[rows, :] = d[:, 0:128] + d[:, 128:256]
        return carry

    lax.fori_loop(0, depth // 256, turn_rows, 0)

    for copy in pending:
        copy.wait_send()
    for line, ahead, index, place in lines:

        @pl.when(ahead != 0)
        def _():
            remote(
                part.at[line], rsbuf.at[index, place], rssend.at[line], rsrecv.at[index, place], peer(ahead)
            ).wait_send()


def per_device(weight, factor, pairing):
    pair = jnp.concatenate([pairing, pairing + BLOCK], axis=1)
    rows, depth = weight.shape
    vmem = pl.BlockSpec(memory_space=pltpu.VMEM)
    f32, b16 = jnp.float32, jnp.bfloat16
    dma = pltpu.SemaphoreType.DMA
    n_gram = len(GRAM)
    rotated, right = pl.pallas_call(
        kernel,
        out_shape=(jax.ShapeDtypeStruct((16, 2, 8, 128), f32), jax.ShapeDtypeStruct((depth, 128), f32)),
        in_specs=[vmem, pl.BlockSpec(memory_space=pl.ANY), vmem],
        out_specs=(vmem, vmem),
        scratch_shapes=[
            pltpu.VMEM((NX * NZ * NY, 2 * rows, depth // 2), b16),
            pltpu.VMEM((5, depth, 128), b16),
            pltpu.VMEM((NX * NZ, NY * rows, 256), f32),
            pltpu.VMEM((3, NZ, NY * rows, 256), f32),
            pltpu.VMEM((2, 128, 128), f32),
            pltpu.VMEM((4, 2, 128, 128), f32),
            pltpu.VMEM((8, 256, 256), f32),
            pltpu.VMEM((n_gram, 128), f32),
            pltpu.VMEM((4, n_gram, 128), f32),
            pltpu.VMEM((8, 128, 256), b16),
            pltpu.VMEM((8, 128, 128), f32),
            pltpu.VMEM((16, 128), f32),
            dma((len(TREE),)),
            dma((len(TREE),)),
            dma,
            dma((7,)),
            dma((7,)),
            dma((8,)),
            dma((3, NZ)),
            dma((7,)),
            dma((4, 2)),
            dma((3,)),
            dma((4,)),
        ],
        compiler_params=pltpu.CompilerParams(
            collective_id=0, has_side_effects=True, vmem_limit_bytes=48 * 2**20
        ),
        name="whiten_turn",
    )(weight, factor, pair)
    return rotated.reshape(256, 128), right


def solution(mesh):
    in_specs = (P("blk", "rows"), P("rows", "blk"), P())
    out_specs = (P("rows", "blk"), P("rows", "blk"))
    return jax.shard_map(per_device, mesh=mesh, in_specs=in_specs, out_specs=out_specs, check_vma=False)
```

time: 417 us -> 120 us (0.29)
  the two profiles are of different devices: /device:TPU:128 before, /device:TPU:74 now
where the time goes in v1:
time: 120 us
  Pallas kernels  114 us (95%)
  local copies, waits for them, and re-layouts  4.04 us (3%)
  other arithmetic  1.44 us (1%)
    pallas_call x1, Pallas kernels, per_device(): pl.pallas_call(kernel, out_shape=(jax.ShapeDtypeStruct((16, 2, 8, 128), f...  114 us
    unnamed x6, local copies, waits for them, and re-layouts  4.04 us

profile of v1, /device:TPU:74, one launch (start us, length us, event | category | flops | bytes accessed | tf_op | source)
XLA Modules:
  0.0 119.9 jit_solution(8553352511502474993)
XLA Ops:
  0.6 0.7 broadcast_add_fusion
  1.3 0.8 pad_add_fusion.pair_ref
  2.1 0.0 copy-start
  2.1 1.2 %copy-done = bf16[4096,128]{1,0:T(8,128)(2,1)S(1)} copy-done((bf16[4096,128]{1,0:T(8,128)(2,1)S(1)}, bf16[4096,128]{1,0:T(8,128)(2,1)}, u32[]{:S(2)}) %copy-start) | copy-done | bytes 1048600
  3.3 0.0 copy-start.1
  3.3 0.8 copy-done.1
  4.1 113.8 %whiten_turn.1 = (f32[16,2,8,128]{3,2,1,0:T(8,128)S(1)}, f32[4096,128]{1,0:T(8,128)S(1)}) custom-call(bf16[8,4096]{1,0:T(8,128)(2,1)S(1)} %copy-done.1, bf16[4096,128]{1,0:T(8,128)(2,1)S(1)} %copy-done, s32[4,128]{1,0:T(4,128)S(1)} %pad_add_fusion.pair_ref), custom_call_target="tpu_custom_call" | custom-call | tf_op jit(solution)/shard_map/whiten_turn/pallas_call | solution.py:416
  117.9 0.7 copy.7
  118.6 1.3 %copy.8 = f32[4096,128]{1,0:T(8,128)} copy(f32[4096,128]{1,0:T(8,128)S(1)} %get-tuple-element.9) | data formatting | bytes 4194304
Async XLA Ops:
  2.1 1.2 %copy-start = (bf16[4096,128]{1,0:T(8,128)(2,1)S(1)}, bf16[4096,128]{1,0:T(8,128)(2,1)}, u32[]{:S(2)}) copy-start(bf16[4096,128]{1,0:T(8,128)(2,1)} %f_ref.1) | copy-start | bytes 3145732
  3.3 0.8 copy-start.1

commit v2 on v1

v2 whole, which is shorter than its diff:
```python
import functools
import jax
import jax.numpy as jnp
from jax import lax
from jax.experimental import pallas as pl
from jax.experimental.pallas import tpu as pltpu
from jax.sharding import PartitionSpec as P

MESH = pl.DeviceIdType.MESH
BLOCK = 64
STEPS = 4
NX, NZ, NY, NR = 4, 2, 8, 4
NB = 2 * NX * NZ * NY
HALF = NY // 2
HOPS = ((1, 0, 0), (3, 0, 0), (0, 1, 0), (0, 0, 1), (0, 0, 3))
TREE = (
    (0, 1, 0, 2), (3, 0, 0, 1), (1, 0, 0, 0), (0, 0, 3, 4), (0, 0, 1, 3), (2, 0, 0, 1), (1, 1, 0, 2), (3, 1, 0, 1),
    (1, 0, 3, 4), (0, 1, 1, 2), (1, 0, 1, 0), (3, 0, 3, 1), (2, 1, 0, 0), (0, 1, 3, 2), (3, 0, 1, 1), (0, 0, 2, 3),
    (1, 1, 1, 0), (2, 0, 3, 0), (2, 0, 1, 1), (0, 1, 2, 2), (1, 0, 2, 0), (3, 1, 1, 1), (2, 1, 1, 0), (3, 1, 3, 1),
    (2, 1, 3, 2), (3, 1, 2, 1), (2, 0, 2, 0), (1, 1, 2, 0), (1, 1, 3, 1), (2, 1, 2, 1), (3, 0, 2, 0),
)
LEAVES = tuple((b3, b2, b1) for b3 in (0, 1) for b2 in (0, 1) for b1 in (0, 1))


def plus(offset, hop):
    return tuple((a + b) % n for a, b, n in zip(offset, hop, (NX, NZ, HALF)))


def block_moves(which):
    sigma = 1 - 2 * (which % 2)
    pair = 1 - 2 * (which // 2)
    kinds, own = [], []
    for kind, base in enumerate((0, sigma, 2 * pair + sigma, 2 * pair)):
        moves = [(base + delta, (3 - delta) // 2) for delta in (1, -1, 3, -3)]
        own += [(kind, place) for shift, place in moves if shift == 0]
        kinds.append([(shift, place) for shift, place in moves if shift != 0])
    return kinds, own


MOVES = [block_moves(which) for which in range(4)]
SENDERS = [
    sorted(
        -shift
        for which in range(4)
        for kind in MOVES[which][0]
        for shift, _ in kind
        if (which + shift) % 4 == receiver
    )
    for receiver in range(4)
]


def turn(p_minus_r, q):
    y = 2.0 * q
    x = p_minus_r
    top = jnp.maximum(jnp.abs(x), jnp.abs(y))
    safe = jnp.where(top > 0.0, top, 1.0)
    xs = jnp.where(top > 0.0, x / safe, 1.0)
    ys = jnp.where(top > 0.0, y / safe, 0.0)
    h = jnp.sqrt(xs * xs + ys * ys)
    big = jnp.sqrt(0.5 * (1.0 + jnp.abs(xs) / h))
    small = jnp.abs(ys) / (2.0 * h * big)
    cosine = jnp.where(x >= 0.0, big, small)
    size = jnp.where(x >= 0.0, small, big)
    return cosine, jnp.where(y < 0.0, -size, size)


def split3(x):
    hi = x.astype(jnp.bfloat16)
    rest = x - hi.astype(jnp.float32)
    mid = rest.astype(jnp.bfloat16)
    low = (rest - mid.astype(jnp.float32)).astype(jnp.bfloat16)
    return hi, mid, low


def dot(a, b, dims=(((1,), (0,)), ((), ()))):
    return lax.dot_general(a, b, dims, preferred_element_type=jnp.float32)


def gram_plan():
    rows = {}
    for n in range(8):
        rows["pr", n] = len(rows)
        rows["q", n] = len(rows)
    for level in (1, 2, 3):
        for n in range(8):
            for m in range(8):
                if n >> level == m >> level and (n >> (level - 1)) & 1 == 0 and (m >> (level - 1)) & 1 == 1:
                    rows["same", n, m] = len(rows)
                    rows["cross", n, m] = len(rows)
    return rows


GRAM = gram_plan()


def kernel(
    w_hbm, f_ref, pair_hbm, rot_ref, right_ref,
    w_ref, pair_ref, wbuf, fbuf, part, rsbuf, part2, rsbuf2, wsum, xbuf, ybuf, gram, gbuf, ebuf, mbuf, coef,
    wsend, wrecv, w_sem, pair_sem, own_sem, fsend, frecv, rssend, rsrecv, rs2send, rs2recv, xsend, xrecv, gsend, grecv,
):
    b = lax.axis_index("blk")
    r = lax.axis_index("rows")
    core = lax.rem(b, 2)
    y = lax.rem(b // 2, NY)
    z = lax.rem(b // (2 * NY), NZ)
    x = b // (2 * NY * NZ)
    sigma = 1 - 2 * core
    odd = lax.rem(y, 2)
    yy = y // 2
    tau = sigma * (1 - 2 * odd)
    which = lax.rem(b, 4)

    def pick(values):
        if len(set(values)) == 1:
            return values[0]
        out = jnp.int32(values[0])
        for k in (1, 2, 3):
            out = jnp.where(which == k, values[k], out)
        return out

    def blk(shift):
        return (lax.rem(b + shift + NB, NB), r)

    def hop(h):
        dx, dz, dy = HOPS[h]
        index = lax.rem(x + dx, NX) * (2 * NY * NZ) + lax.rem(z + dz, NZ) * (2 * NY) + (lax.rem(yy + dy, HALF) * 2 + odd) * 2 + core
        return (index, r)

    def peer(shift):
        return (b, lax.rem(r + shift, NR))

    own_weight = pltpu.make_async_copy(w_hbm, w_ref, w_sem)
    own_weight.start()
    own_pairing = pltpu.make_async_copy(pair_hbm, pair_ref, pair_sem)
    own_pairing.start()
    own_factor = pltpu.make_async_copy(f_ref, fbuf.at[0], own_sem)
    own_factor.start()

    barrier = pltpu.get_barrier_semaphore()
    greet = [hop(h) for h in range(5)] + [peer(s) for s in (1, 2, 3)]
    greet += [blk(sigma * s) for s in (1, -1, 3, -3)]
    greet += [blk(pick([SENDERS[w][k] for w in range(4)])) for k in range(len(SENDERS[0]))]
    for target in greet:
        pl.semaphore_signal(barrier, inc=1, device_id=target, device_id_type=MESH)

    def remote(src, dst, send, recv, target):
        return pltpu.make_async_remote_copy(
            src_ref=src, dst_ref=dst, send_sem=send, recv_sem=recv, device_id=target, device_id_type=MESH
        )

    def slot(offset):
        return (offset[0] * NZ + offset[1]) * HALF + offset[2]

    index_of = {entry[:3]: k for k, entry in enumerate(TREE)}
    children = {}
    for k, entry in enumerate(TREE):
        back = tuple(-v for v in HOPS[entry[3]])
        children.setdefault(plus(entry[:3], back), []).append(k)
    pending = []

    def weight_copy(k):
        offset, h = TREE[k][:3], TREE[k][3]
        source = plus(offset, tuple(-v for v in HOPS[h]))
        return remote(wbuf.at[slot(source)], wbuf.at[slot(offset)], wsend.at[k], wrecv.at[k], hop(h))

    def forward(offset):
        for k in children.get(offset, ()):
            copy = weight_copy(k)
            copy.start()
            pending.append(copy)

    def arrived(k):
        weight_copy(k).wait_recv()

    own_weight.wait()
    wide = w_ref[...].astype(jnp.float32)
    half = wide.shape[1] // 2
    wbuf[0] = jnp.concatenate([wide[:, :half], wide[:, half:]], axis=0).astype(jnp.bfloat16)

    pl.semaphore_wait(barrier, len(greet))
    forward((0, 0, 0))
    own_factor.wait()
    swap = remote(fbuf.at[0], fbuf.at[1], fsend.at[0], frecv.at[0], blk(sigma))
    swap.start()
    pending.append(swap)

    depth = fbuf.shape[1]
    halves = [pl.ds(0, depth // 2), pl.ds(depth // 2, depth // 2)]
    moves = ((1, -1, 2), (3, 3, 4))
    near = jnp.where(tau > 0, 4, 2)

    def factor_copy(which_move, k):
        base, shift, place = moves[which_move]
        return remote(
            fbuf.at[0, halves[k]],
            fbuf.at[place, halves[k]],
            fsend.at[base + k],
            frecv.at[base + k],
            blk(sigma * shift),
        )

    def far_copy(k):
        return remote(
            fbuf.at[0, halves[k]], fbuf.at[3, halves[k]], fsend.at[5 + k], frecv.at[5 + k], blk(-3 * sigma)
        )

    def share_copy(k):
        return remote(fbuf.at[near, halves[k]], fbuf.at[5, halves[k]], fsend.at[7 + k], frecv.at[7 + k], blk(sigma))

    for k in (0, 1):
        for which_move in (0, 1):
            copy = factor_copy(which_move, k)
            copy.start()
            pending.append(copy)

    def share(k):
        @pl.when(tau > 0)
        def _():
            factor_copy(1, k).wait_recv()

        @pl.when(tau < 0)
        def _():
            factor_copy(0, k).wait_recv()

        copy = share_copy(k)
        copy.start()
        pending.append(copy)

    own_pairing.wait()

    row_id = lax.broadcasted_iota(jnp.int32, (128, 128), 0)
    lane_id = lax.broadcasted_iota(jnp.int32, (128, 128), 1)

    def exact(mask):
        return jnp.where(mask, 1.0, 0.0).astype(jnp.bfloat16)

    pairs = pair_ref[...]
    wide_pair = jnp.concatenate([pairs, pairs + BLOCK], axis=1)
    turns = [exact(row_id == wide_pair[s : s + 1, :]) for s in range(STEPS)]
    eye = exact(row_id == lane_id)
    swap_halves = exact(lax.rem(row_id + BLOCK, 2 * BLOCK) == lane_id)
    low_lane = lane_id < BLOCK
    first = jnp.where(low_lane, eye.astype(jnp.float32), turns[0].astype(jnp.float32)).astype(jnp.bfloat16)
    last = jnp.where(low_lane, eye.astype(jnp.float32), turns[3].astype(jnp.float32)).astype(jnp.bfloat16)
    across = (((1,), (1,)), ((), ()))
    down = (((0,), (0,)), ((), ()))
    q1, q2, q3 = (dot(turns[s - 1], turns[s], down).astype(jnp.bfloat16) for s in (1, 2, 3))
    for n, (b3, b2, b1) in enumerate(LEAVES):
        m = eye
        for bit, q in ((b3, q3), (b2, q2), (b1, q1)):
            if bit:
                m = dot(q, m).astype(jnp.bfloat16)
        e = dot(first, m)
        es = dot(e.astype(jnp.bfloat16), swap_halves)
        ebuf[n, :, 0:128] = e.astype(jnp.bfloat16)
        ebuf[n, :, 128:256] = es.astype(jnp.bfloat16)
        mbuf[n] = dot((e + es).astype(jnp.bfloat16), last, across)


    waited = set()
    kdim = half
    groups = []

    def product(left, first_block, second_block, sides):
        count = left.shape[0] // 16
        total = None
        for side in sides:
            rows = pl.ds(side * kdim, kdim)
            right = jnp.concatenate([fbuf[first_block, rows, :], fbuf[second_block, rows, :]], axis=1)
            d = dot(left, right).reshape(count, 2, 8, 256)[:, side]
            total = d if total is None else total + d
        return total.reshape(count * 8, 256)

    def send_sums(dx, src, dst, send, recv):
        ahead = lax.rem(x - dx - r + 2 * NX, NR)
        index = jnp.maximum(ahead - 1, 0)
        copy = remote(src, dst(index), send, recv(index), peer(ahead))

        @pl.when(ahead != 0)
        def _():
            copy.start()

        groups.append((ahead, copy))

    def whiten(line):
        dx, dz = line // NZ, line % NZ
        for dy in range(HALF):
            if (dx, dz, dy) != (0, 0, 0) and index_of[dx, dz, dy] not in waited:
                arrived(index_of[dx, dz, dy])
                waited.add(index_of[dx, dz, dy])
        left = wbuf[pl.ds(line * HALF, HALF)].reshape(HALF * 16, kdim)
        part[line] = product(left, 0, 1, (0, 1))
        send_sums(
            dx,
            part.at[line],
            lambda index: rsbuf.at[index, dz],
            rssend.at[line],
            lambda index: rsrecv.at[index, dz],
        )

    mine = lax.rem(x - r + NX, NX)

    def row_place(dz, dy):
        at = lax.rem(z + dz, NZ) * 32 + lax.rem(yy - dy + HALF, HALF) * 8
        return pl.ds(pl.multiple_of(at, 8), 8)

    def sum_own():
        for dz in range(NZ):
            for k in range(3):
                remote(part.at[0], rsbuf.at[k, dz], rssend.at[0], rsrecv.at[k, dz], peer(1)).wait_recv()
            total = (part[mine * NZ + dz] + rsbuf[0, dz]) + (rsbuf[1, dz] + rsbuf[2, dz])
            for dy in range(HALF):
                wsum[0, row_place(dz, dy), :] = total[8 * dy : 8 * dy + 8, 0:128]
                wsum[1, row_place(dz, dy), :] = total[8 * dy : 8 * dy + 8, 128:256]

    def whiten_partner(dx):
        left = wbuf[pl.ds(dx * NZ * HALF, NZ * HALF)].reshape(NZ * HALF * 16, kdim)
        part2[dx] = product(left, near, 5, (0, 1))
        send_sums(dx, part2.at[dx], lambda index: rsbuf2.at[index], rs2send.at[dx], lambda index: rs2recv.at[index])

    def sum_partner():
        for k in range(3):
            remote(part2.at[0], rsbuf2.at[k], rs2send.at[0], rs2recv.at[k], peer(1)).wait_recv()
        total = (part2[mine] + rsbuf2[0]) + (rsbuf2[1] + rsbuf2[2])
        for dz in range(NZ):
            for dy in range(HALF):
                at = (dz * HALF + dy) * 8
                wsum[2, row_place(dz, dy), :] = total[at : at + 8, 0:128]
                wsum[3, row_place(dz, dy), :] = total[at : at + 8, 128:256]

    def block_out(kinds):
        for kind in kinds:
            for k in range(len(MOVES[0][0][kind])):
                shift = pick([MOVES[w][0][kind][k][0] for w in range(4)])
                place = pick([MOVES[w][0][kind][k][1] for w in range(4)])
                copy = remote(
                    wsum.at[kind],
                    xbuf.at[place, core, odd],
                    xsend.at[kind, k],
                    xrecv.at[place, core, odd],
                    blk(shift),
                )
                copy.start()
                pending.append(copy)
            for k in range(2):
                if MOVES[0][1][k][0] == kind:
                    place = pick([MOVES[w][1][k][1] for w in range(4)])
                    xbuf[place, core, odd] = wsum[kind]

    events = []
    for line in range(NX * NZ):
        last_index = max(index_of.get((line // NZ, line % NZ, dy), -1) for dy in range(HALF))
        events.append((last_index, 1, line))
    for k, entry in enumerate(TREE):
        if entry[:3] in children:
            events.append((k, 0, k))
    events.sort()
    begun = False
    for _, kind, a in events:
        if kind == 0:
            arrived(a)
            waited.add(a)
            forward(TREE[a][:3])
        else:
            if not begun:
                swap.wait_recv()
                begun = True
            whiten(a)
    for k in (0, 1):
        copy = far_copy(k)
        copy.start()
        pending.append(copy)
    for k in (0, 1):
        share(k)
    sum_own()
    block_out((0, 1))
    for k in (0, 1):
        share_copy(k).wait_recv()
    for dx in range(NX):
        whiten_partner(dx)
    sum_partner()
    block_out((2, 3))
    taken = [pick([MOVES[w][1][k][1] for w in range(4)]) for k in range(2)]
    for place in range(4):
        for kind in range(2):
            for side in range(2):
                here = jnp.logical_and(kind == core, side == odd)
                here = jnp.logical_and(here, jnp.logical_or(place == taken[0], place == taken[1]))

                @pl.when(jnp.logical_not(here))
                def _():
                    remote(
                        wsum.at[0], xbuf.at[place, kind, side], xsend.at[0, 0], xrecv.at[place, kind, side], blk(sigma)
                    ).wait_recv()

    for i in range(4):
        pieces = split3(xbuf[i].reshape(256, 128))
        for n in range(8):
            if sum(LEAVES[n]) == i:
                e = ebuf[n]
                ybuf[n] = dot(pieces[0], e) + dot(pieces[1], e) + dot(pieces[2], e)

    def put(name, a, c):
        k = GRAM[name]
        gram[k : k + 1, :] = jnp.sum(a * c, axis=0, keepdims=True)

    for n in range(8):
        a = ybuf[n, :, 0:128]
        put(("pr", n), a, a)
        put(("q", n), a, ybuf[n, :, 128:256])
        for m in range(8):
            if ("same", n, m) in GRAM:
                put(("same", n, m), a, ybuf[m, :, 0:128])
                put(("cross", n, m), a, ybuf[m, :, 128:256])
    gbuf[r] = gram[...]
    for shift in (1, 2, 3):
        copy = remote(gram, gbuf.at[r], gsend.at[shift - 1], grecv.at[r], peer(shift))
        copy.start()
        pending.append(copy)
    for shift in (1, 2, 3):
        other = lax.rem(r + shift, NR)
        remote(gram, gbuf.at[other], gsend.at[0], grecv.at[other], peer(shift)).wait_recv()
    gram_sum = (gbuf[0] + gbuf[1]) + (gbuf[2] + gbuf[3])
    gram_roll = pltpu.roll(gram_sum, BLOCK, 1)

    def row(name, rolled=False):
        k = GRAM[name]
        return (gram_roll if rolled else gram_sum)[k : k + 1, :]

    def rotate(node_u, node_l, p, rr, q):
        c, s = turn(p - rr, q)
        names = sorted(set(node_u) | set(node_l))
        up, low = {}, {}
        for name in names:
            if name in node_u and name in node_l:
                up[name] = c * node_u[name] + s * node_l[name]
                low[name] = c * node_l[name] - s * node_u[name]
            elif name in node_u:
                up[name] = c * node_u[name]
                low[name] = -s * node_u[name]
            else:
                up[name] = s * node_l[name]
                low[name] = c * node_l[name]
        cross = 2.0 * c * s * q
        return up, low, c * c * p + cross + s * s * rr, s * s * p - cross + c * c * rr

    def between(k1, k2):
        n, m = k1 // 2, k2 // 2
        if k1 % 2 == 0:
            return row(("same", n, m)) if k2 % 2 == 0 else row(("cross", n, m))
        return row(("cross", n, m), True) if k2 % 2 == 0 else row(("same", n, m), True)

    one = jnp.ones((1, 128), jnp.float32)
    nodes = [
        rotate({2 * n: one}, {2 * n + 1: one}, row(("pr", n)), row(("pr", n), True), row(("q", n))) for n in range(8)
    ]
    for level in (1, 2, 3):
        grown = []
        for k in range(0, len(nodes), 2):
            up, low = nodes[k][0], nodes[k + 1][1]
            q = None
            for k1, c1 in up.items():
                inner = None
                for k2, c2 in low.items():
                    term = c2 * between(k1, k2)
                    inner = term if inner is None else inner + term
                q = c1 * inner if q is None else q + c1 * inner
            grown.append(rotate(up, low, nodes[k][2], nodes[k + 1][3], q))
        nodes = grown
    up, low = nodes[0][0], nodes[0][1]
    low_row = lax.broadcasted_iota(jnp.int32, (1, 128), 1) < BLOCK
    for k in range(16):
        coef[k : k + 1, :] = jnp.where(low_row, up[k], pltpu.roll(low[k], BLOCK, 1))
    spread = sum(dot(piece, last, across) for piece in split3(coef[...]))
    upper_rows = row_id < BLOCK
    t = [None] * 4
    for n in range(8):
        term = mbuf[n] * jnp.where(upper_rows, spread[2 * n : 2 * n + 1, :], spread[2 * n + 1 : 2 * n + 2, :])
        i = sum(LEAVES[n])
        t[i] = term if t[i] is None else t[i] + term

    rotated = None
    pieces_t = [split3(v) for v in t]
    for i in range(4):
        xs = split3(xbuf[i].reshape(256, 128))
        for a in range(3):
            for c in range(3 - a):
                term = dot(xs[a], pieces_t[i][c])
                rotated = term if rotated is None else rotated + term
    for c in range(2):
        for side in range(2):
            at = (c * 2 + side) * 64
            rot_ref[:, side, c] = rotated[at : at + 64].reshape(8, 8, 128)

    pair_t = [jnp.concatenate([v[0], v[1]], axis=1) for v in pieces_t]
    even = core == 0

    def choose(a, c):
        return jnp.where(even, a.astype(jnp.float32), c.astype(jnp.float32)).astype(jnp.bfloat16)

    t_cat = jnp.concatenate(
        [
            choose(pair_t[2], pair_t[1]),
            choose(pair_t[1], pair_t[2]),
            choose(pair_t[0], pair_t[3]),
            choose(pair_t[3], pair_t[0]),
        ],
        axis=0,
    )
    for k in (0, 1):

        @pl.when(tau < 0)
        def _():
            factor_copy(1, k).wait_recv()

        @pl.when(tau > 0)
        def _():
            factor_copy(0, k).wait_recv()

        far_copy(k).wait_recv()

    def turn_rows(k, carry):
        rows = pl.ds(pl.multiple_of(k * 512, 512), 512)
        left = jnp.concatenate([fbuf[s, rows, :] for s in (1, 2, 3, 4)], axis=1)
        d = dot(left, t_cat)
        right_ref[rows, :] = d[:, 0:128] + d[:, 128:256]
        return carry

    lax.fori_loop(0, depth // 512, turn_rows, 0)

    for copy in pending:
        copy.wait_send()
    for ahead, copy in groups:

        @pl.when(ahead != 0)
        def _():
            copy.wait_send()


def per_device(weight, factor, pairing):
    rows, depth = weight.shape
    vmem = pl.BlockSpec(memory_space=pltpu.VMEM)
    f32, b16 = jnp.float32, jnp.bfloat16
    dma = pltpu.SemaphoreType.DMA
    n_gram = len(GRAM)
    rotated, right = pl.pallas_call(
        kernel,
        out_shape=(jax.ShapeDtypeStruct((8, 2, 2, 8, 128), f32), jax.ShapeDtypeStruct((depth, 128), f32)),
        in_specs=[pl.BlockSpec(memory_space=pltpu.HBM)] * 3,
        out_specs=(vmem, vmem),
        scratch_shapes=[
            pltpu.VMEM((rows, depth), b16),
            pltpu.VMEM(pairing.shape, jnp.int32),
            pltpu.VMEM((NX * NZ * HALF, 2 * rows, depth // 2), b16),
            pltpu.VMEM((6, depth, 128), b16),
            pltpu.VMEM((NX * NZ, HALF * rows, 256), f32),
            pltpu.VMEM((3, NZ, HALF * rows, 256), f32),
            pltpu.VMEM((NX, NZ * HALF * rows, 256), f32),
            pltpu.VMEM((3, NZ * HALF * rows, 256), f32),
            pltpu.VMEM((4, 64, 128), f32),
            pltpu.VMEM((4, 2, 2, 64, 128), f32),
            pltpu.VMEM((8, 256, 256), f32),
            pltpu.VMEM((n_gram, 128), f32),
            pltpu.VMEM((4, n_gram, 128), f32),
            pltpu.VMEM((8, 128, 256), b16),
            pltpu.VMEM((8, 128, 128), f32),
            pltpu.VMEM((16, 128), f32),
            dma((len(TREE),)),
            dma((len(TREE),)),
            dma,
            dma,
            dma,
            dma((9,)),
            dma((9,)),
            dma((NX * NZ,)),
            dma((3, NZ)),
            dma((NX,)),
            dma((3,)),
            dma((4, 4)),
            dma((4, 2, 2)),
            dma((3,)),
            dma((4,)),
        ],
        compiler_params=pltpu.CompilerParams(
            collective_id=0, has_side_effects=True, vmem_limit_bytes=60 * 2**20
        ),
        name="whiten_turn",
    )(weight, factor, pairing)
    return rotated.reshape(256, 128), right


def solution(mesh):
    in_specs = (P("blk", "rows"), P("rows", "blk"), P())
    out_specs = (P("rows", "blk"), P("rows", "blk"))
    return jax.shard_map(per_device, mesh=mesh, in_specs=in_specs, out_specs=out_specs, check_vma=False)
```

time: 120 us -> 111 us (0.925)
  the two profiles are of different devices: /device:TPU:74 before, /device:TPU:23 now
where the time goes in v2:
time: 111 us
  Pallas kernels  105 us (95%)
  local copies, waits for them, and re-layouts  4.61 us (4%)
    pallas_call x1, Pallas kernels, per_device(): pl.pallas_call(kernel, out_shape=(jax.ShapeDtypeStruct((8, 2, 2, 8, 128),...  105 us
    unnamed x2, local copies, waits for them, and re-layouts  4.61 us

profile of v2, /device:TPU:23, one launch (start us, length us, event | category | flops | bytes accessed | tf_op | source)
XLA Modules:
  0.0 110.6 jit_solution(15066963062200575816)
XLA Ops:
  0.6 105.3 %whiten_turn.1 = (f32[8,2,2,8,128]{4,3,2,1,0:T(8,128)}, f32[4096,128]{1,0:T(8,128)}) custom-call(bf16[8,4096]{1,0:T(8,128)(2,1)} %w_hbm.1, bf16[4096,128]{1,0:T(8,128)(2,1)} %f_ref.1, s32[4,64]{1,0:T(4,128)} %pair_hbm.1), custom_call_target="tpu_custom_call" | custom-call | tf_op jit(solution)/shard_map/whiten_turn/pallas_call | solution.py:547
  106.0 1.6 %copy.7 = f32[256,128]{1,0:T(8,128)} copy(f32[256,128]{1,0:T(8,128)} %bitcast.1) | data formatting | bytes 262144
  107.6 3.0 %copy.8 = f32[4096,128]{1,0:T(8,128)} copy(f32[4096,128]{1,0:T(8,128)} %get-tuple-element.9) | data formatting | bytes 4194304

commit v3 on v2

--- a/solution.py
+++ b/solution.py
@@ -508,18 +508,6 @@
         ],
         axis=0,
     )
-    for k in (0, 1):
-
-        @pl.when(tau < 0)
-        def _():
-            factor_copy(1, k).wait_recv()
-
-        @pl.when(tau > 0)
-        def _():
-            factor_copy(0, k).wait_recv()
-
-        far_copy(k).wait_recv()
-
     def turn_rows(k, carry):
         rows = pl.ds(pl.multiple_of(k * 512, 512), 512)
         left = jnp.concatenate([fbuf[s, rows, :] for s in (1, 2, 3, 4)], axis=1)
@@ -527,7 +515,19 @@
         right_ref[rows, :] = d[:, 0:128] + d[:, 128:256]
         return carry
 
-    lax.fori_loop(0, depth // 512, turn_rows, 0)
+    for k in (0, 1):
+
+        @pl.when(tau < 0)
+        def _():
+            factor_copy(1, k).wait_recv()
+
+        @pl.when(tau > 0)
+        def _():
+            factor_copy(0, k).wait_recv()
+
+        far_copy(k).wait_recv()
+        steps = depth // 1024
+        lax.fori_loop(k * steps, (k + 1) * steps, turn_rows, 0)
 
     for copy in pending:
         copy.wait_send()

time: 111 us -> 111 us (level)
  no operation moved by 1% of the time
where the time goes in v3:
time: 111 us
  Pallas kernels  105 us (95%)
  local copies, waits for them, and re-layouts  4.61 us (4%)
    pallas_call x1, Pallas kernels, per_device(): pl.pallas_call(kernel, out_shape=(jax.ShapeDtypeStruct((8, 2, 2, 8, 128),...  105 us
    unnamed x2, local copies, waits for them, and re-layouts  4.61 us

profile of v3, /device:TPU:23, one launch (start us, length us, event | category | flops | bytes accessed | tf_op | source)
XLA Modules:
  0.0 110.6 jit_solution(5699062111433308585)
XLA Ops:
  0.6 105.3 %whiten_turn.1 = (f32[8,2,2,8,128]{4,3,2,1,0:T(8,128)}, f32[4096,128]{1,0:T(8,128)}) custom-call(bf16[8,4096]{1,0:T(8,128)(2,1)} %w_hbm.1, bf16[4096,128]{1,0:T(8,128)(2,1)} %f_ref.1, s32[4,64]{1,0:T(4,128)} %pair_hbm.1), custom_call_target="tpu_custom_call" | custom-call | tf_op jit(solution)/shard_map/whiten_turn/pallas_call | solution.py:547
  106.0 1.6 %copy.7 = f32[256,128]{1,0:T(8,128)} copy(f32[256,128]{1,0:T(8,128)} %bitcast.1) | data formatting | bytes 262144
  107.5 3.0 %copy.8 = f32[4096,128]{1,0:T(8,128)} copy(f32[4096,128]{1,0:T(8,128)} %get-tuple-element.9) | data formatting | bytes 4194304
